TPU v7x, 128 devices: a whole 4x4x4 slice. The times are simulated.
128 devices in a mesh: ctx: 8 (over y, z_hi), rep: 16 (over x, z_lo, core).
Axes of the slice: x: 4, y: 4, z: 4 (z_hi: 2, z_lo: 2; z = z_hi * 2 + z_lo), core: 2. Of those that a mesh axis runs over, the one named last changes fastest.
Arguments:
- queries: bfloat16 [16, 4096, 8192], P('rep', 'ctx'), may hold values from -20 to 20
- keys: bfloat16 [16, 4096, 1024], P('rep', 'ctx'), may hold values from -20 to 20
- values: bfloat16 [16, 4096, 1024], P('rep', 'ctx'), may hold values from -6 to 6
- doc_lengths: int32 [16, 16], replicated, may hold values from 1 to 1024, 4096 in all within a row
Outputs:
- attended: bfloat16 [16, 4096, 8192], P('rep', 'ctx')
All inputs are finite; a program needn't handle non-finite values.
Results may differ from a plain program's by a relative error of at most 0.0075.
Values may be sent and summed in bfloat16 or wider, within the bound.
A program may use at most 192 MiB of HBM per device.

v0:
```python
import jax
import jax.numpy as jnp
from jax import lax
from jax.sharding import PartitionSpec as P

HQ = 64
KEY_HEADS = 8
HEAD_SIZE = 128
QUERY_PER_KEY = 8


def shifted(block, axis, distance):
    devices = range(lax.axis_size(axis))
    route = [(i - distance, i) for i in devices if i - distance in devices]
    return lax.ppermute(block, axis, route)


def swapped(value, axis, distance):
    return lax.ppermute(value, axis, [(i, i ^ 1 << distance) for i in range(lax.axis_size(axis))])


def shortened(value):

    def short(part):
        return part.astype(jnp.bfloat16) if part.dtype == jnp.float32 else part

    return jax.tree.map(short, value)


def segment_info(doc_lengths, replica, start, block_count):
    doc_row = lax.dynamic_index_in_dim(doc_lengths, replica, 0, keepdims=False)
    doc_ends = jnp.cumsum(doc_row)
    doc_starts = doc_ends - doc_row
    positions = start + jnp.arange(block_count, dtype=jnp.int32)
    segment = jnp.sum((positions[:, None] >= doc_ends[None, :]).astype(jnp.int32), axis=1)
    doc_first = jnp.max(
        jnp.where(doc_starts[None, :] <= positions[:, None], doc_starts[None, :], 0), axis=1
    )
    return (positions, segment, doc_first)


def empty_state(block_count):
    return (
        jnp.full((KEY_HEADS, QUERY_PER_KEY, block_count), -1e30, jnp.float32),
        jnp.zeros((KEY_HEADS, QUERY_PER_KEY, block_count), jnp.float32),
        jnp.zeros((KEY_HEADS, QUERY_PER_KEY, block_count, HEAD_SIZE), jnp.float32),
    )


def pass_blocks(key_tile_rows, value_tile_rows):
    return shifted((key_tile_rows, value_tile_rows), "ctx", 1)


def attend_tile(
    state,
    query_tile,
    query_positions,
    query_segment,
    key_tile_rows,
    value_tile_rows,
    key_positions,
    key_segment,
    enabled,
):
    mask = (key_positions[None, :] <= query_positions[:, None]) & (
        key_segment[None, :] == query_segment[:, None]
    )
    mask = mask & (key_positions[None, :] >= 0)
    live = enabled & jnp.any(mask)
    heads_of_key = key_tile_rows.reshape(key_tile_rows.shape[0], KEY_HEADS, HEAD_SIZE)
    heads_of_value = value_tile_rows.reshape(value_tile_rows.shape[0], KEY_HEADS, HEAD_SIZE)

    def update(carry):
        run_max, run_sum, run_out = carry
        scores = jnp.einsum(
            "qhgd,khd->hgqk", query_tile, heads_of_key, preferred_element_type=jnp.float32
        ) * HEAD_SIZE ** (-0.5)
        scores = jnp.where(mask[None, None], scores, -1e30)
        new_max = jnp.maximum(run_max, jnp.max(scores, axis=-1))
        weights = jnp.where(mask[None, None], jnp.exp(scores - new_max[..., None]), 0.0)
        factor = jnp.exp(run_max - new_max)
        new_sum = run_sum * factor + jnp.sum(weights, axis=-1)
        new_out = run_out * factor[..., None] + jnp.einsum(
            "hgqk,khd->hgqd",
            weights.astype(jnp.bfloat16),
            heads_of_value,
            preferred_element_type=jnp.float32,
        )
        return (new_max, new_sum, new_out)

    def keep(carry):
        return carry

    return lax.cond(live, update, keep, state)


def attend(
    state,
    query_tile,
    query_positions,
    query_segment,
    key_tile_rows,
    value_tile_rows,
    key_positions,
    key_segment,
    enabled,
):
    key_half = key_tile_rows.shape[0] // 2
    for tile_index in range(2):
        offset = tile_index * key_half
        state = attend_tile(
            state,
            query_tile,
            query_positions,
            query_segment,
            key_tile_rows[offset : offset + key_half],
            value_tile_rows[offset : offset + key_half],
            key_positions[offset : offset + key_half],
            key_segment[offset : offset + key_half],
            enabled,
        )
    return state


def finish(state):
    run_max, run_sum, run_out = state
    output = run_out / run_sum[..., None]
    block_count = output.shape[2]
    return (
        jnp.transpose(output, (2, 0, 1, 3))
        .reshape(block_count, HQ * HEAD_SIZE)
        .astype(jnp.bfloat16)
    )


def on_device(queries, keys, values, doc_lengths):
    length_total = queries.shape[1]
    half_length = length_total // 2
    rep_index = lax.axis_index("rep")
    ctx_index = lax.axis_index("ctx")
    loop_size = lax.axis_size("ctx")
    seq_total = length_total * loop_size
    steps = min(loop_size, (seq_total // 4 - 2 + length_total) // length_total + 1)
    heads_of_query = queries[0].reshape(length_total, KEY_HEADS, QUERY_PER_KEY, HEAD_SIZE)
    first_half = heads_of_query[:half_length]
    second_half = heads_of_query[half_length:]
    positions, segment, doc_first = segment_info(
        doc_lengths, rep_index, ctx_index * length_total, length_total
    )
    key_tile_rows = keys[0]
    value_tile_rows = values[0]
    first_state = empty_state(half_length)
    second_state = empty_state(half_length)
    always = jnp.array(True)
    bit = 0
    partner = jnp.bitwise_xor(rep_index, 1 << bit)
    own_work = jnp.sum(positions - doc_first + 1)
    other_positions, other_segment, other_first = segment_info(
        doc_lengths, partner, ctx_index * length_total, length_total
    )
    other_work = jnp.sum(other_positions - other_first + 1)
    self_heavy = own_work > other_work
    other_heavy = other_work > own_work
    borrowed_work = swapped(queries[0, half_length:], "rep", bit)
    borrowed_work = borrowed_work.reshape(half_length, KEY_HEADS, QUERY_PER_KEY, HEAD_SIZE)
    lent_state = empty_state(half_length)
    for step in range(steps):
        source = ctx_index - step
        key_positions, key_segment, unused = segment_info(
            doc_lengths, rep_index, source * length_total, length_total
        )
        first_state = attend(
            first_state,
            first_half,
            positions[:half_length],
            segment[:half_length],
            key_tile_rows,
            value_tile_rows,
            key_positions,
            key_segment,
            always,
        )
        second_state = attend(
            second_state,
            second_half,
            positions[half_length:],
            segment[half_length:],
            key_tile_rows,
            value_tile_rows,
            key_positions,
            key_segment,
            jnp.logical_not(self_heavy),
        )
        other_keys, other_values = swapped((key_tile_rows, value_tile_rows), "rep", bit)
        other_key_positions, other_key_segment, unused = segment_info(
            doc_lengths, partner, source * length_total, length_total
        )
        lent_state = attend(
            lent_state,
            borrowed_work,
            other_positions[half_length:],
            other_segment[half_length:],
            other_keys,
            other_values,
            other_key_positions,
            other_key_segment,
            other_heavy,
        )
        if step < steps - 1:
            key_tile_rows, value_tile_rows = pass_blocks(key_tile_rows, value_tile_rows)
    returned = jax.tree.map(
        lambda part, own: part.astype(own.dtype),
        swapped(shortened(lent_state), "rep", bit),
        lent_state,
    )

    def pick_state(from_partner, kept_here):
        return jnp.where(self_heavy, from_partner, kept_here)

    second_state = jax.tree.map(pick_state, tuple(returned), second_state)
    second_rows = finish(second_state)
    output = jnp.concatenate([finish(first_state), second_rows], axis=0)
    return output[None]


def solution(mesh):
    return jax.shard_map(
        on_device,
        mesh=mesh,
        in_specs=(P("rep", "ctx", None), P("rep", "ctx", None), P("rep", "ctx", None), P()),
        out_specs=P("rep", "ctx", None),
        check_vma=False,
    )
```

profile of v0, /device:TPU:66, one launch (start us, length us, event | category | flops | bytes accessed | tf_op | source)
XLA Modules:
  0.0 553.0 jit_solution(12315866240181566987)
XLA Ops:
  0.0 6.1 %fusion.367 = (bf16[1,256,8192]{2,1,0:T(8,128)(2,1)}, bf16[1,256,8192]{2,1,0:T(8,128)(2,1)}) fusion(bf16[1,512,8192]{2,1,0:T(8,128)(2,1)} %param.40), kind=kLoop, calls=%fused_computation.440 | loop fusion | bytes 16777216 | tf_op jit(solution)/shard_map/slice | solution.py:145
  6.1 6.4 %copy.348 = bf16[1,256,8192]{1,2,0:T(8,128)(2,1)} copy(bf16[1,256,8192]{2,1,0:T(8,128)(2,1)} %get-tuple-element.926) | data formatting | bytes 8388608
  16.5 5.8 %collective-permute-start.1 = (bf16[512,1024]{0,1:T(8,128)(2,1)S(1)}, bf16[512,1024]{0,1:T(8,128)(2,1)}, u32[]{:S(2)}, u32[]{:S(2)}) collective-permute-start(bf16[512,1024]{0,1:T(8,128)(2,1)S(1)} %bitcast.557), channel_id=1, source_target_pairs={{0,16},{16,32},{32,48},{48,64},{64,80},{80,96},{96,112},{1,17},{17... | collective-permute-start | bytes 3145736 | tf_op jit(solution)/shard_map/ppermute | solution.py:15
  24.7 17.8 %collective-permute-done = bf16[512,1024]{0,1:T(8,128)(2,1)} collective-permute-done((bf16[512,1024]{0,1:T(8,128)(2,1)S(1)}, bf16[512,1024]{0,1:T(8,128)(2,1)}, u32[]{:S(2)}, u32[]{:S(2)}) %collective-permute-start) | collective-permute-done | bytes 1048608 | tf_op jit(solution)/shard_map/ppermute | solution.py:15
  46.0 19.0 %collective-permute-done.1 = bf16[512,1024]{0,1:T(8,128)(2,1)} collective-permute-done((bf16[512,1024]{0,1:T(8,128)(2,1)S(1)}, bf16[512,1024]{0,1:T(8,128)(2,1)}, u32[]{:S(2)}, u32[]{:S(2)}) %collective-permute-start.1) | collective-permute-done | bytes 1048608 | tf_op jit(solution)/shard_map/ppermute | solution.py:15
  80.2 29.4 %collective-permute-done.3 = bf16[512,1024]{0,1:T(8,128)(2,1)} collective-permute-done((bf16[512,1024]{0,1:T(8,128)(2,1)}, bf16[512,1024]{0,1:T(8,128)(2,1)}, u32[]{:S(2)}, u32[]{:S(2)}) %collective-permute-start.3) | collective-permute-done | bytes 1048608 | tf_op jit(solution)/shard_map/ppermute | solution.py:15
  116.6 31.9 %conditional.24 = (f32[8,8,256]{2,1,0:T(8,128)}, f32[8,8,256]{2,1,0:T(8,128)S(1)}, f32[8,8,256,128]{3,2,1,0:T(8,128)}) conditional(s32[]{:T(128)} %convert_element_type.178, () %tuple.130, (pred[256,256]{0,1:T(8,128)(4,1)}, bf16[256,8,128]{0,2,1:T(8,128)(2,1)S(1)}, bf16[256,8,8,128]{0,3,2,1:T(8,128)(2,1)}, ...), branch_computations={%region_48.49_spmd, %region_49.52_spmd} | conditional | flops 2204172288 | bytes 65142836 | solution.py:94
  117.2 9.6 %fusion.109 = (f32[8,8,256]{2,1,0:T(8,128)S(1)}, f32[8,256,256,8]{2,1,3,0:T(8,128)}) fusion(pred[256,256]{0,1:T(8,128)(4,1)} %get-tuple-element.370, bf16[256,8,8,128]{0,3,2,1:T(8,128)(2,1)} %get-tuple-element.733, bf16[256,8,128]{0,2,1:T(8,128)(2,1)S(1)} %get-tuple-element.732), kind=kOutput, calls=%fused_computation.123 | convolution fusion | flops 1086308352 | bytes 21626880 | tf_op jit(solution)/shard_map/cond/branch_1_fun/qhgd,khd->hgqk/dot_general | solution.py:75
  127.4 12.2 %broadcast_add_fusion.1 = f32[8,8,256,128]{3,2,1,0:T(8,128)} fusion(f32[8,8,256]{2,1,0:T(8,128)S(1)} %get-tuple-element.835, f32[8,256,256,8]{2,1,3,0:T(8,128)} %get-tuple-element.902, f32[8,8,256]{2,1,0:T(8,128)} %get-tuple-element.1086, pred[256,256]{0,1:T(8,128)(4,1)S(1)} %copy-done.33, bf16[256,8,128]{0,2,1:T(8,128)(2,1)S(1)} %get-tuple-element.734), kind=kOutput, calls=%fused_computation.132 | convolution fusion | flops 1096810496 | bytes 25886720 | tf_op jit(solution)/shard_map/cond/branch_1_fun/hgqk,khd->hgqd/dot_general | solution.py:83
  139.6 8.0 %fusion.111 = f32[8,8,256]{2,1,0:T(8,128)S(1)} fusion(f32[8,256,256,8]{2,1,3,0:T(8,128)} %get-tuple-element.902, f32[8,8,256]{2,1,0:T(8,128)} %get-tuple-element.1086, pred[256,256]{0,1:T(8,128)(4,1)S(1)} %copy-done.33), kind=kLoop, calls=%fused_computation.125 | loop fusion | flops 20955136 | bytes 16973824 | tf_op jit(solution)/shard_map/cond/branch_1_fun/reduce_sum | solution.py:82
  148.5 30.1 %conditional.25 = ((f32[8,8,256]{2,1,0:T(8,128)}, f32[8,8,256]{2,1,0:T(8,128)S(1)}, f32[8,8,256,128]{3,2,1,0:T(8,128)})) conditional(s32[]{:T(128)} %convert_element_type.177, (f32[8,8,256]{2,1,0:T(8,128)}, f32[8,8,256]{2,1,0:T(8,128)S(1)}, f32[8,8,256,128]{3,2,1,0:T(8,128)}) %conditional.24, (pred[256,256]{0,1:T(8,128)(4,1)S(1)}, ...), branch_computations={%region_52.53_spmd, %region_53.56_spmd} | conditional | flops 2206236672 | bytes 142803040 | solution.py:94
  164.4 13.6 %multiply_add_fusion.10 = f32[8,8,256,128]{3,2,1,0:T(8,128)} fusion(f32[8,8,256,128]{3,2,1,0:T(8,128)} %get-tuple-element.379, f32[8,8,256]{2,1,0:T(8,128)S(1)} %get-tuple-element.838, f32[8,256,256,8]{2,1,3,0:T(8,128)} %copy-done.2, f32[8,8,256]{2,1,0:T(8,128)S(1)} %max.35, pred[256,256]{0,1:T(8,128)(4,1)S(1)} %get-tuple-element.375, ...), kind=kOutput, calls=%fused_computation.148 | convolution fusion | flops 1098907648 | bytes 34275328 | tf_op jit(solution)/shard_map/cond/branch_1_fun/hgqk,khd->hgqd/dot_general | solution.py:83
  178.6 30.2 %conditional.26 = ((f32[8,8,256]{2,1,0:T(8,128)}, f32[8,8,256]{2,1,0:T(8,128)S(1)}, f32[8,8,256,128]{3,2,1,0:T(8,128)})) conditional(s32[]{:T(128)} %convert_element_type.176, (f32[8,8,256]{2,1,0:T(8,128)}, f32[8,8,256]{2,1,0:T(8,128)S(1)}, f32[8,8,256,128]{3,2,1,0:T(8,128)}) %get-tuple-element.1156, (pred[256,256]{0,1:T(8,128)(4,1)S(1)}, ...), branch_computations={%region_56.57_spmd, %region_57.60_spmd} | conditional | flops 2206236672 | bytes 140705856 | solution.py:94
  194.6 13.6 %multiply_add_fusion.12 = f32[8,8,256,128]{3,2,1,0:T(8,128)} fusion(f32[8,8,256,128]{3,2,1,0:T(8,128)} %get-tuple-element.386, f32[8,8,256]{2,1,0:T(8,128)S(1)} %get-tuple-element.840, f32[8,256,256,8]{2,1,3,0:T(8,128)} %copy-done.3, f32[8,8,256]{2,1,0:T(8,128)S(1)} %max.36, pred[256,256]{0,1:T(8,128)(4,1)S(1)} %get-tuple-element.382, ...), kind=kOutput, calls=%fused_computation.168 | convolution fusion | flops 1098907648 | bytes 34275328 | tf_op jit(solution)/shard_map/cond/branch_1_fun/hgqk,khd->hgqd/dot_general | solution.py:83
  208.8 30.0 %conditional.27 = ((f32[8,8,256]{2,1,0:T(8,128)}, f32[8,8,256]{2,1,0:T(8,128)S(1)}, f32[8,8,256,128]{3,2,1,0:T(8,128)})) conditional(s32[]{:T(128)} %convert_element_type.175, (f32[8,8,256]{2,1,0:T(8,128)}, f32[8,8,256]{2,1,0:T(8,128)S(1)}, f32[8,8,256,128]{3,2,1,0:T(8,128)}) %get-tuple-element.1157, (pred[256,256]{0,1:T(8,128)(4,1)S(1)}, ...), branch_computations={%region_60.61_spmd, %region_61.64_spmd} | conditional | flops 2206236672 | bytes 140705856 | solution.py:94
  224.6 13.6 %multiply_add_fusion.14 = f32[8,8,256,128]{3,2,1,0:T(8,128)} fusion(f32[8,8,256,128]{3,2,1,0:T(8,128)} %get-tuple-element.393, f32[8,8,256]{2,1,0:T(8,128)S(1)} %get-tuple-element.842, f32[8,256,256,8]{2,1,3,0:T(8,128)} %copy-done.4, f32[8,8,256]{2,1,0:T(8,128)S(1)} %max.37, pred[256,256]{0,1:T(8,128)(4,1)S(1)} %get-tuple-element.389, ...), kind=kOutput, calls=%fused_computation.188 | convolution fusion | flops 1098907648 | bytes 34275328 | tf_op jit(solution)/shard_map/cond/branch_1_fun/hgqk,khd->hgqd/dot_general | solution.py:83
  239.1 6.6 %conditional.29 = ((f32[8,8,256]{2,1,0:T(8,128)S(1)}, f32[8,8,256,128]{3,2,1,0:T(8,128)})) conditional(s32[]{:T(128)} %convert_element_type.172, (f32[8,8,256]{2,1,0:T(8,128)S(1)}, f32[8,8,256,128]{3,2,1,0:T(8,128)}) %tuple.136, (pred[256,256]{0,1:T(8,128)(4,1)S(1)}, bf16[512,1024]{0,1:T(8,128)(2,1)}, bf16[256,8,8,128]{0,3,2,1:T(8,128)(2,1)}, ...), branch_computations={%region_68.69_spmd, %region_69.72_spmd} | conditional | flops 2206236672 | bytes 142671936 | solution.py:94
  245.7 6.3 %convert_element_type.179 = bf16[8,8,256,128]{3,2,1,0:T(8,128)(2,1)} convert(f32[8,8,256,128]{3,2,1,0:T(8,128)} %get-tuple-element.531) | non-fusion elementwise | flops 2097152 | bytes 12582912 | tf_op jit(solution)/shard_map/convert_element_type | solution.py:25
  253.2 6.4 %copy.347 = bf16[1,256,8192]{1,2,0:T(8,128)(2,1)} copy(bf16[1,256,8192]{2,1,0:T(8,128)(2,1)} %get-tuple-element.925) | data formatting | bytes 8388608
  268.3 31.5 %conditional.18 = (f32[8,8,256]{2,1,0:T(8,128)}, f32[8,8,256]{2,1,0:T(8,128)S(1)}, f32[8,8,256,128]{3,2,1,0:T(8,128)}) conditional(s32[]{:T(128)} %convert_element_type.166, () %tuple.122, (pred[256,256]{0,1:T(8,128)(4,1)S(1)}, bf16[256,8,128]{0,2,1:T(8,128)(2,1)S(1)}, bf16[256,8,8,128]{0,3,2,1:T(8,128)(2,1)}, ...), branch_computations={%region_10.11_spmd, %region_11.14_spmd} | conditional | flops 2204172288 | bytes 64880664 | solution.py:94
  268.5 9.7 %fusion = (f32[8,8,256]{2,1,0:T(8,128)S(1)}, f32[8,256,256,8]{2,1,3,0:T(8,128)}) fusion(pred[256,256]{0,1:T(8,128)(4,1)S(1)} %get-tuple-element.331, bf16[256,8,8,128]{0,3,2,1:T(8,128)(2,1)} %get-tuple-element.694, bf16[256,8,128]{0,2,1:T(8,128)(2,1)S(1)} %get-tuple-element.693), kind=kOutput, calls=%fused_computation.2 | convolution fusion | flops 1086308352 | bytes 21626880 | tf_op jit(solution)/shard_map/cond/branch_1_fun/qhgd,khd->hgqk/dot_general | solution.py:75
  278.8 12.2 %broadcast_add_fusion = f32[8,8,256,128]{3,2,1,0:T(8,128)} fusion(f32[8,8,256]{2,1,0:T(8,128)S(1)} %get-tuple-element.823, f32[8,256,256,8]{2,1,3,0:T(8,128)} %get-tuple-element.890, f32[8,8,256]{2,1,0:T(8,128)} %get-tuple-element.1120, pred[256,256]{0,1:T(8,128)(4,1)S(1)} %get-tuple-element.331, bf16[256,8,128]{0,2,1:T(8,128)(2,1)} %get-tuple-element.695), kind=kOutput, calls=%fused_computation.11 | convolution fusion | flops 1096810496 | bytes 25886720 | tf_op jit(solution)/shard_map/cond/branch_1_fun/hgqk,khd->hgqd/dot_general | solution.py:83
  291.0 8.0 %fusion.2 = f32[8,8,256]{2,1,0:T(8,128)S(1)} fusion(f32[8,256,256,8]{2,1,3,0:T(8,128)} %get-tuple-element.890, f32[8,8,256]{2,1,0:T(8,128)} %get-tuple-element.1120, pred[256,256]{0,1:T(8,128)(4,1)S(1)} %get-tuple-element.331), kind=kLoop, calls=%fused_computation.4 | loop fusion | flops 20955136 | bytes 16973824 | tf_op jit(solution)/shard_map/cond/branch_1_fun/reduce_sum | solution.py:82
  300.7 35.7 %conditional.30 = (f32[8,8,256]{2,1,0:T(8,128)}, f32[8,8,256]{2,1,0:T(8,128)S(1)}, f32[8,8,256,128]{3,2,1,0:T(8,128)}) conditional(s32[]{:T(128)} %convert_element_type.186, () %tuple.138, (pred[256,256]{0,1:T(8,128)(4,1)S(1)}, bf16[256,8,128]{0,2,1:T(8,128)(2,1)S(1)}, bf16[256,8,8,128]{0,3,2,1:T(8,128)(2,1)}, ...), branch_computations={%region_78.79_spmd, %region_79.82_spmd} | conditional | flops 2204172288 | bytes 64880664 | solution.py:94
  305.1 9.6 %fusion.212 = (f32[8,8,256]{2,1,0:T(8,128)S(1)}, f32[8,256,256,8]{2,1,3,0:T(8,128)}) fusion(pred[256,256]{0,1:T(8,128)(4,1)S(1)} %get-tuple-element.409, bf16[256,8,8,128]{0,3,2,1:T(8,128)(2,1)} %get-tuple-element.772, bf16[256,8,128]{0,2,1:T(8,128)(2,1)S(1)} %get-tuple-element.771), kind=kOutput, calls=%fused_computation.238 | convolution fusion | flops 1086308352 | bytes 21626880 | tf_op jit(solution)/shard_map/cond/branch_1_fun/qhgd,khd->hgqk/dot_general | solution.py:75
  315.3 12.2 %broadcast_add_fusion.2 = f32[8,8,256,128]{3,2,1,0:T(8,128)} fusion(f32[8,8,256]{2,1,0:T(8,128)S(1)} %get-tuple-element.847, f32[8,256,256,8]{2,1,3,0:T(8,128)} %get-tuple-element.914, f32[8,8,256]{2,1,0:T(8,128)} %get-tuple-element.1052, pred[256,256]{0,1:T(8,128)(4,1)S(1)} %get-tuple-element.409, bf16[256,8,128]{0,2,1:T(8,128)(2,1)} %get-tuple-element.773), kind=kOutput, calls=%fused_computation.247 | convolution fusion | flops 1096810496 | bytes 25886720 | tf_op jit(solution)/shard_map/cond/branch_1_fun/hgqk,khd->hgqd/dot_general | solution.py:83
  327.6 8.0 %fusion.214 = f32[8,8,256]{2,1,0:T(8,128)S(1)} fusion(f32[8,256,256,8]{2,1,3,0:T(8,128)} %get-tuple-element.914, f32[8,8,256]{2,1,0:T(8,128)} %get-tuple-element.1052, pred[256,256]{0,1:T(8,128)(4,1)S(1)} %get-tuple-element.409), kind=kLoop, calls=%fused_computation.240 | loop fusion | flops 20955136 | bytes 16973824 | tf_op jit(solution)/shard_map/cond/branch_1_fun/reduce_sum | solution.py:82
  336.5 30.1 %conditional.31 = ((f32[8,8,256]{2,1,0:T(8,128)}, f32[8,8,256]{2,1,0:T(8,128)S(1)}, f32[8,8,256,128]{3,2,1,0:T(8,128)})) conditional(s32[]{:T(128)} %convert_element_type.185, (f32[8,8,256]{2,1,0:T(8,128)}, f32[8,8,256]{2,1,0:T(8,128)S(1)}, f32[8,8,256,128]{3,2,1,0:T(8,128)}) %conditional.30, (pred[256,256]{0,1:T(8,128)(4,1)S(1)}, ...), branch_computations={%region_82.83_spmd, %region_83.86_spmd} | conditional | flops 2206236672 | bytes 140705856 | solution.py:94
  342.3 4.9 copy-done.6
  352.3 13.6 %multiply_add_fusion.20 = f32[8,8,256,128]{3,2,1,0:T(8,128)} fusion(f32[8,8,256,128]{3,2,1,0:T(8,128)} %get-tuple-element.418, f32[8,8,256]{2,1,0:T(8,128)S(1)} %get-tuple-element.850, f32[8,256,256,8]{2,1,3,0:T(8,128)} %copy-done.6, f32[8,8,256]{2,1,0:T(8,128)S(1)} %max.40, pred[256,256]{0,1:T(8,128)(4,1)S(1)} %get-tuple-element.414, ...), kind=kOutput, calls=%fused_computation.263 | convolution fusion | flops 1098907648 | bytes 34275328 | tf_op jit(solution)/shard_map/cond/branch_1_fun/hgqk,khd->hgqd/dot_general | solution.py:83
  369.1 30.2 %conditional.20 = ((f32[8,8,256]{2,1,0:T(8,128)}, f32[8,8,256]{2,1,0:T(8,128)S(1)}, f32[8,8,256,128]{3,2,1,0:T(8,128)})) conditional(s32[]{:T(128)} %convert_element_type.164, (f32[8,8,256]{2,1,0:T(8,128)}, f32[8,8,256]{2,1,0:T(8,128)S(1)}, f32[8,8,256,128]{3,2,1,0:T(8,128)}) %get-tuple-element.1151, (pred[256,256]{0,1:T(8,128)(4,1)S(1)}, ...), branch_computations={%region_18.19_spmd, %region_19.22_spmd} | conditional | flops 2206236672 | bytes 140705856 | solution.py:94
  375.2 4.9 copy-done.7
  385.2 13.5 %multiply_add_fusion.2 = f32[8,8,256,128]{3,2,1,0:T(8,128)} fusion(f32[8,8,256,128]{3,2,1,0:T(8,128)} %get-tuple-element.347, f32[8,8,256]{2,1,0:T(8,128)S(1)} %get-tuple-element.828, f32[8,256,256,8]{2,1,3,0:T(8,128)} %copy-done.7, f32[8,8,256]{2,1,0:T(8,128)S(1)} %max.31, pred[256,256]{0,1:T(8,128)(4,1)S(1)} %get-tuple-element.343, ...), kind=kOutput, calls=%fused_computation.47 | convolution fusion | flops 1098907648 | bytes 34275328 | tf_op jit(solution)/shard_map/cond/branch_1_fun/hgqk,khd->hgqd/dot_general | solution.py:83
  399.3 29.9 %conditional.21 = ((f32[8,8,256]{2,1,0:T(8,128)}, f32[8,8,256]{2,1,0:T(8,128)S(1)}, f32[8,8,256,128]{3,2,1,0:T(8,128)})) conditional(s32[]{:T(128)} %convert_element_type.163, (f32[8,8,256]{2,1,0:T(8,128)}, f32[8,8,256]{2,1,0:T(8,128)S(1)}, f32[8,8,256,128]{3,2,1,0:T(8,128)}) %get-tuple-element.1152, (pred[256,256]{0,1:T(8,128)(4,1)S(1)}, ...), branch_computations={%region_22.23_spmd, %region_23.26_spmd} | conditional | flops 2206236672 | bytes 140705856 | solution.py:94
  405.0 4.9 copy-done.8
  415.0 13.5 %multiply_add_fusion.4 = f32[8,8,256,128]{3,2,1,0:T(8,128)} fusion(f32[8,8,256,128]{3,2,1,0:T(8,128)} %get-tuple-element.354, f32[8,8,256]{2,1,0:T(8,128)S(1)} %get-tuple-element.830, f32[8,256,256,8]{2,1,3,0:T(8,128)} %copy-done.8, f32[8,8,256]{2,1,0:T(8,128)S(1)} %max.32, pred[256,256]{0,1:T(8,128)(4,1)S(1)} %get-tuple-element.350, ...), kind=kOutput, calls=%fused_computation.67 | convolution fusion | flops 1098907648 | bytes 34275328 | tf_op jit(solution)/shard_map/cond/branch_1_fun/hgqk,khd->hgqd/dot_general | solution.py:83
  429.2 30.2 %conditional.32 = ((f32[8,8,256]{2,1,0:T(8,128)}, f32[8,8,256]{2,1,0:T(8,128)S(1)}, f32[8,8,256,128]{3,2,1,0:T(8,128)})) conditional(s32[]{:T(128)} %convert_element_type.184, (f32[8,8,256]{2,1,0:T(8,128)}, f32[8,8,256]{2,1,0:T(8,128)S(1)}, f32[8,8,256,128]{3,2,1,0:T(8,128)}) %get-tuple-element.1161, (pred[256,256]{0,1:T(8,128)(4,1)S(1)}, ...), branch_computations={%region_86.87_spmd, %region_87.90_spmd} | conditional | flops 2206236672 | bytes 140705856 | solution.py:94
  434.9 4.9 copy-done.9
  445.2 13.6 %multiply_add_fusion.22 = f32[8,8,256,128]{3,2,1,0:T(8,128)} fusion(f32[8,8,256,128]{3,2,1,0:T(8,128)} %get-tuple-element.425, f32[8,8,256]{2,1,0:T(8,128)S(1)} %get-tuple-element.852, f32[8,256,256,8]{2,1,3,0:T(8,128)} %copy-done.9, f32[8,8,256]{2,1,0:T(8,128)S(1)} %max.41, pred[256,256]{0,1:T(8,128)(4,1)S(1)} %get-tuple-element.421, ...), kind=kOutput, calls=%fused_computation.283 | convolution fusion | flops 1098907648 | bytes 34275328 | tf_op jit(solution)/shard_map/cond/branch_1_fun/hgqk,khd->hgqd/dot_general | solution.py:83
  459.4 30.2 %conditional.33 = ((f32[8,8,256]{2,1,0:T(8,128)}, f32[8,8,256]{2,1,0:T(8,128)S(1)}, f32[8,8,256,128]{3,2,1,0:T(8,128)})) conditional(s32[]{:T(128)} %convert_element_type.183, (f32[8,8,256]{2,1,0:T(8,128)}, f32[8,8,256]{2,1,0:T(8,128)S(1)}, f32[8,8,256,128]{3,2,1,0:T(8,128)}) %get-tuple-element.1162, (pred[256,256]{0,1:T(8,128)(4,1)S(1)}, ...), branch_computations={%region_90.91_spmd, %region_91.94_spmd} | conditional | flops 2206236672 | bytes 140705856 | solution.py:94
  465.2 4.9 copy-done.10
  475.4 13.6 %multiply_add_fusion.24 = f32[8,8,256,128]{3,2,1,0:T(8,128)} fusion(f32[8,8,256,128]{3,2,1,0:T(8,128)} %get-tuple-element.432, f32[8,8,256]{2,1,0:T(8,128)S(1)} %get-tuple-element.854, f32[8,256,256,8]{2,1,3,0:T(8,128)} %copy-done.10, f32[8,8,256]{2,1,0:T(8,128)S(1)} %max.42, pred[256,256]{0,1:T(8,128)(4,1)S(1)} %get-tuple-element.428, ...), kind=kOutput, calls=%fused_computation.303 | convolution fusion | flops 1098907648 | bytes 34275328 | tf_op jit(solution)/shard_map/cond/branch_1_fun/hgqk,khd->hgqd/dot_general | solution.py:83
  493.0 5.2 conditional.23
  498.4 12.0 %fusion.321 = bf16[256,8,8,128]{3,0,2,1:T(8,128)(2,1)S(1)} fusion(f32[8,8,256,128]{3,2,1,0:T(8,128)} %get-tuple-element.514, f32[8,8,256]{2,1,0:T(8,128)S(1)} %get-tuple-element.515), kind=kLoop, calls=%fused_computation.362 | loop fusion | flops 4194304 | bytes 12648448 | tf_op jit(solution)/shard_map/convert_element_type | solution.py:132
  513.1 10.1 %copy.354 = bf16[32,8,64,128]{3,1,2,0:T(8,128)(2,1)} copy(bf16[32,8,64,128]{3,2,1,0:T(8,128)(2,1)S(1)} %bitcast.539) | data formatting | bytes 8388608
  524.1 8.0 %fusion.322 = bf16[256,8,8,128]{3,0,2,1:T(8,128)(2,1)S(1)} fusion(f32[8,8,256]{2,1,0:T(8,128)S(1)} %convert_select_fusion, f32[8,8,256,128]{3,2,1,0:T(8,128)} %get-tuple-element.547, bf16[8,8,256,128]{3,2,1,0:T(8,128)(2,1)} %collective-permute-done.11, pred[]{:T(512)S(6)} %gt.6), kind=kLoop, calls=%fused_computation.363 | loop fusion | flops 8388608 | bytes 16842752 | tf_op jit(solution)/shard_map/convert_element_type | solution.py:132
  534.9 10.1 %copy.353 = bf16[32,8,64,128]{3,1,2,0:T(8,128)(2,1)} copy(bf16[32,8,64,128]{3,2,1,0:T(8,128)(2,1)S(1)} %bitcast.540) | data formatting | bytes 8388608
  545.0 7.9 %maximum_bitcast_fusion = bf16[1,512,8192]{2,1,0:T(8,128)(2,1)} fusion(bf16[256,8192]{1,0:T(8,128)(2,1)} %bitcast.542, bf16[256,8192]{1,0:T(8,128)(2,1)} %bitcast.541), kind=kLoop, calls=%fused_computation.357 | loop fusion | flops 16777216 | bytes 16777216 | tf_op jit(solution)/shard_map/broadcast_in_dim | solution.py:223
  (170 shorter events, 151.0 us)
Async XLA Ops:
  0.0 12.5 %copy-start.34 = (bf16[1,512,1024]{2,1,0:T(8,128)(2,1)S(1)}, bf16[1,512,1024]{2,1,0:T(8,128)(2,1)}, u32[]{:S(2)}) copy-start(bf16[1,512,1024]{2,1,0:T(8,128)(2,1)} %param.41) | copy-start | bytes 3145732
  0.0 16.0 %copy-start.35 = (bf16[1,512,1024]{2,1,0:T(8,128)(2,1)S(1)}, bf16[1,512,1024]{2,1,0:T(8,128)(2,1)}, u32[]{:S(2)}) copy-start(bf16[1,512,1024]{2,1,0:T(8,128)(2,1)} %param.42) | copy-start | bytes 3145732
  12.5 104.0 %collective-permute-start.5 = (bf16[256,8192]{0,1:T(8,128)(2,1)}, bf16[256,8192]{0,1:T(8,128)(2,1)}, u32[]{:S(2)}, u32[]{:S(2)}) collective-permute-start(bf16[256,8192]{0,1:T(8,128)(2,1)} %bitcast.526), channel_id=1, source_target_pairs={{0,1},{1,0},{2,3},{3,2},{4,5},{5,4},{6,7},{7,6},{8,9},{9,8},{10,11... | collective-permute-start | bytes 12582920 | tf_op jit(solution)/shard_map/ppermute | solution.py:19
  13.1 103.5 %copy-start.15 = (bf16[1,512,1024]{1,2,0:T(8,128)(2,1)}, bf16[1,512,1024]{1,2,0:T(8,128)(2,1)S(1)}, u32[]{:S(2)}) copy-start(bf16[1,512,1024]{1,2,0:T(8,128)(2,1)S(1)} %copy.142) | copy-start | bytes 3145732
  13.1 29.5 %collective-permute-start = (bf16[512,1024]{0,1:T(8,128)(2,1)S(1)}, bf16[512,1024]{0,1:T(8,128)(2,1)}, u32[]{:S(2)}, u32[]{:S(2)}) collective-permute-start(bf16[512,1024]{0,1:T(8,128)(2,1)S(1)} %bitcast.555), channel_id=1, source_target_pairs={{0,16},{16,32},{32,48},{48,64},{64,80},{80,96},{96,112},{1,17},{17... | collective-permute-start | bytes 3145736 | tf_op jit(solution)/shard_map/ppermute | solution.py:15
  15.7 56.1 %collective-permute-start.4 = (bf16[512,1024]{0,1:T(8,128)(2,1)S(1)}, bf16[512,1024]{0,1:T(8,128)(2,1)}, u32[]{:S(2)}, u32[]{:S(2)}) collective-permute-start(bf16[512,1024]{0,1:T(8,128)(2,1)S(1)} %bitcast.556), channel_id=1, source_target_pairs={{0,1},{1,0},{2,3},{3,2},{4,5},{5,4},{6,7},{7,6},{8,9},{9,8},{10,11... | collective-permute-start | bytes 3145736 | tf_op jit(solution)/shard_map/ppermute | solution.py:19
  16.5 100.1 %copy-start.17 = (bf16[1,512,1024]{1,2,0:T(8,128)(2,1)}, bf16[1,512,1024]{1,2,0:T(8,128)(2,1)S(1)}, u32[]{:S(2)}) copy-start(bf16[1,512,1024]{1,2,0:T(8,128)(2,1)S(1)} %copy.144) | copy-start | bytes 3145732
  16.5 48.5 %collective-permute-start.1 = (bf16[512,1024]{0,1:T(8,128)(2,1)S(1)}, bf16[512,1024]{0,1:T(8,128)(2,1)}, u32[]{:S(2)}, u32[]{:S(2)}) collective-permute-start(bf16[512,1024]{0,1:T(8,128)(2,1)S(1)} %bitcast.557), channel_id=1, source_target_pairs={{0,16},{16,32},{32,48},{48,64},{64,80},{80,96},{96,112},{1,17},{17... | collective-permute-start | bytes 3145736 | tf_op jit(solution)/shard_map/ppermute | solution.py:15
  22.3 49.4 %collective-permute-start.6 = (bf16[512,1024]{0,1:T(8,128)(2,1)S(1)}, bf16[512,1024]{0,1:T(8,128)(2,1)S(1)}, u32[]{:S(2)}, u32[]{:S(2)}) collective-permute-start(bf16[512,1024]{0,1:T(8,128)(2,1)S(1)} %bitcast.558), channel_id=1, source_target_pairs={{0,1},{1,0},{2,3},{3,2},{4,5},{5,4},{6,7},{7,6},{8,9},{9,8},{10,11... | collective-permute-start | bytes 3145736 | tf_op jit(solution)/shard_map/ppermute | solution.py:19
  42.6 67.0 %collective-permute-start.2 = (bf16[512,1024]{0,1:T(8,128)(2,1)}, bf16[512,1024]{0,1:T(8,128)(2,1)}, u32[]{:S(2)}, u32[]{:S(2)}) collective-permute-start(bf16[512,1024]{0,1:T(8,128)(2,1)} %collective-permute-done), channel_id=1, source_target_pairs={{0,16},{16,32},{32,48},{48,64},{64,80},{80,96},{96,112},{1,17},{17... | collective-permute-start | bytes 3145736 | tf_op jit(solution)/shard_map/ppermute | solution.py:15
  65.0 44.6 %collective-permute-start.3 = (bf16[512,1024]{0,1:T(8,128)(2,1)}, bf16[512,1024]{0,1:T(8,128)(2,1)}, u32[]{:S(2)}, u32[]{:S(2)}) collective-permute-start(bf16[512,1024]{0,1:T(8,128)(2,1)} %collective-permute-done.1), channel_id=1, source_target_pairs={{0,16},{16,32},{32,48},{48,64},{64,80},{80,96},{96,112},{1,17},{17... | collective-permute-start | bytes 3145736 | tf_op jit(solution)/shard_map/ppermute | solution.py:15
  71.7 41.3 %collective-permute-start.7 = (bf16[512,1024]{0,1:T(8,128)(2,1)}, bf16[512,1024]{0,1:T(8,128)(2,1)}, u32[]{:S(2)}, u32[]{:S(2)}) collective-permute-start(bf16[512,1024]{0,1:T(8,128)(2,1)} %collective-permute-done), channel_id=1, source_target_pairs={{0,1},{1,0},{2,3},{3,2},{4,5},{5,4},{6,7},{7,6},{8,9},{9,8},{10,11... | collective-permute-start | bytes 3145736 | tf_op jit(solution)/shard_map/ppermute | solution.py:19
  71.8 42.5 %collective-permute-start.8 = (bf16[512,1024]{0,1:T(8,128)(2,1)}, bf16[512,1024]{0,1:T(8,128)(2,1)}, u32[]{:S(2)}, u32[]{:S(2)}) collective-permute-start(bf16[512,1024]{0,1:T(8,128)(2,1)} %collective-permute-done.1), channel_id=1, source_target_pairs={{0,1},{1,0},{2,3},{3,2},{4,5},{5,4},{6,7},{7,6},{8,9},{9,8},{10,11... | collective-permute-start | bytes 3145736 | tf_op jit(solution)/shard_map/ppermute | solution.py:19
  109.6 129.2 %collective-permute-start.10 = (bf16[512,1024]{0,1:T(8,128)(2,1)}, bf16[512,1024]{0,1:T(8,128)(2,1)}, u32[]{:S(2)}, u32[]{:S(2)}) collective-permute-start(bf16[512,1024]{0,1:T(8,128)(2,1)} %collective-permute-done.3), channel_id=1, source_target_pairs={{0,1},{1,0},{2,3},{3,2},{4,5},{5,4},{6,7},{7,6},{8,9},{9,8},{10,11... | collective-permute-start | bytes 3145736 | tf_op jit(solution)/shard_map/ppermute | solution.py:19
  109.6 129.2 %collective-permute-start.9 = (bf16[512,1024]{0,1:T(8,128)(2,1)}, bf16[512,1024]{0,1:T(8,128)(2,1)}, u32[]{:S(2)}, u32[]{:S(2)}) collective-permute-start(bf16[512,1024]{0,1:T(8,128)(2,1)} %collective-permute-done.2), channel_id=1, source_target_pairs={{0,1},{1,0},{2,3},{3,2},{4,5},{5,4},{6,7},{7,6},{8,9},{9,8},{10,11... | collective-permute-start | bytes 3145736 | tf_op jit(solution)/shard_map/ppermute | solution.py:19
  117.1 10.3 %copy-start.33 = (pred[256,256]{0,1:T(8,128)(4,1)S(1)}, pred[256,256]{0,1:T(8,128)(4,1)}, u32[]{:S(2)}) copy-start(pred[256,256]{0,1:T(8,128)(4,1)} %get-tuple-element.370) | copy-start | bytes 196612 | tf_op jit(solution)/shard_map/cond
  148.5 30.2 %copy-start.37 = (bf16[256,1024]{0,1:T(8,128)(2,1)S(1)}, bf16[256,1024]{0,1:T(8,128)(2,1)}, u32[]{:S(2)}) copy-start(bf16[256,1024]{0,1:T(8,128)(2,1)} %get-tuple-element.928) | copy-start | bytes 1572868
  153.5 5.8 %copy-start.2 = (f32[8,256,256,8]{2,1,3,0:T(8,128)}, f32[8,256,256,8]{2,1,3,0:T(8,128)S(1)}, u32[]{:S(2)}) copy-start(f32[8,256,256,8]{2,1,3,0:T(8,128)S(1)} %get-tuple-element.904) | copy-start | bytes 50331652 | tf_op jit(solution)/shard_map/cond
  153.5 10.9 %copy-start.38 = (bf16[256,8,128]{0,2,1:T(8,128)(2,1)S(1)}, bf16[256,8,128]{0,2,1:T(8,128)(2,1)}, u32[]{:S(2)}) copy-start(bf16[256,8,128]{0,2,1:T(8,128)(2,1)} %get-tuple-element.741) | copy-start | bytes 1572868 | tf_op jit(solution)/shard_map/cond
  178.6 30.2 %copy-start.36 = (bf16[256,1024]{0,1:T(8,128)(2,1)S(1)}, bf16[256,1024]{0,1:T(8,128)(2,1)}, u32[]{:S(2)}) copy-start(bf16[256,1024]{0,1:T(8,128)(2,1)} %get-tuple-element.927) | copy-start | bytes 1572868
  183.4 5.8 %copy-start.3 = (f32[8,256,256,8]{2,1,3,0:T(8,128)}, f32[8,256,256,8]{2,1,3,0:T(8,128)S(1)}, u32[]{:S(2)}) copy-start(f32[8,256,256,8]{2,1,3,0:T(8,128)S(1)} %get-tuple-element.906) | copy-start | bytes 50331652 | tf_op jit(solution)/shard_map/cond
  213.6 5.8 %copy-start.4 = (f32[8,256,256,8]{2,1,3,0:T(8,128)}, f32[8,256,256,8]{2,1,3,0:T(8,128)S(1)}, u32[]{:S(2)}) copy-start(f32[8,256,256,8]{2,1,3,0:T(8,128)S(1)} %get-tuple-element.908) | copy-start | bytes 50331652 | tf_op jit(solution)/shard_map/cond
  245.7 22.7 %copy-start.19 = (f32[8,8,256]{2,1,0:T(8,128)}, f32[8,8,256]{2,1,0:T(8,128)S(1)}, u32[]{:S(2)}) copy-start(f32[8,8,256]{2,1,0:T(8,128)S(1)} %get-tuple-element.548) | copy-start | bytes 196612
  245.7 21.7 %copy-start.16 = (bf16[1,512,1024]{1,2,0:T(8,128)(2,1)S(1)}, bf16[1,512,1024]{1,2,0:T(8,128)(2,1)}, u32[]{:S(2)}) copy-start(bf16[1,512,1024]{1,2,0:T(8,128)(2,1)} %copy-done.15) | copy-start | bytes 3145732
  245.7 21.8 %copy-start.18 = (bf16[1,512,1024]{1,2,0:T(8,128)(2,1)S(1)}, bf16[1,512,1024]{1,2,0:T(8,128)(2,1)}, u32[]{:S(2)}) copy-start(bf16[1,512,1024]{1,2,0:T(8,128)(2,1)} %copy-done.17) | copy-start | bytes 3145732
  245.7 22.6 %copy-start.32 = (pred[256,256]{0,1:T(8,128)(4,1)S(1)}, pred[256,256]{0,1:T(8,128)(4,1)}, u32[]{:S(2)}) copy-start(pred[256,256]{0,1:T(8,128)(4,1)} %get-tuple-element.985) | copy-start | bytes 196612
  252.0 272.2 %collective-permute-start.11 = (bf16[8,8,256,128]{3,2,1,0:T(8,128)(2,1)}, bf16[8,8,256,128]{3,2,1,0:T(8,128)(2,1)}, u32[]{:S(2)}, u32[]{:S(2)}) collective-permute-start(bf16[8,8,256,128]{3,2,1,0:T(8,128)(2,1)} %convert_element_type.179), channel_id=1, source_target_pairs={{0,1},{1,0},{2,3},{3,2},{4,5},{5,4},{6,7},{7,6},{8,9},{9,8},{10,11... | collective-permute-start | bytes 12582920 | tf_op jit(solution)/shard_map/ppermute | solution.py:19
  268.3 31.5 %copy-start.31 = (pred[256,256]{0,1:T(8,128)(4,1)S(1)}, pred[256,256]{0,1:T(8,128)(4,1)}, u32[]{:S(2)}) copy-start(pred[256,256]{0,1:T(8,128)(4,1)} %get-tuple-element.982) | copy-start | bytes 196612
  299.9 0.8 copy-start.30
  300.7 35.7 %copy-start.29 = (pred[256,256]{0,1:T(8,128)(4,1)S(1)}, pred[256,256]{0,1:T(8,128)(4,1)}, u32[]{:S(2)}) copy-start(pred[256,256]{0,1:T(8,128)(4,1)} %get-tuple-element.992) | copy-start | bytes 196612
  336.4 32.6 %copy-start.28 = (pred[256,256]{0,1:T(8,128)(4,1)S(1)}, pred[256,256]{0,1:T(8,128)(4,1)}, u32[]{:S(2)}) copy-start(pred[256,256]{0,1:T(8,128)(4,1)} %get-tuple-element.996) | copy-start | bytes 196612
  341.4 5.8 %copy-start.6 = (f32[8,256,256,8]{2,1,3,0:T(8,128)}, f32[8,256,256,8]{2,1,3,0:T(8,128)S(1)}, u32[]{:S(2)}) copy-start(f32[8,256,256,8]{2,1,3,0:T(8,128)S(1)} %get-tuple-element.916) | copy-start | bytes 50331652 | tf_op jit(solution)/shard_map/cond
  369.1 30.3 %copy-start.27 = (pred[256,256]{0,1:T(8,128)(4,1)S(1)}, pred[256,256]{0,1:T(8,128)(4,1)}, u32[]{:S(2)}) copy-start(pred[256,256]{0,1:T(8,128)(4,1)} %get-tuple-element.864) | copy-start | bytes 196612
  374.2 5.8 %copy-start.7 = (f32[8,256,256,8]{2,1,3,0:T(8,128)}, f32[8,256,256,8]{2,1,3,0:T(8,128)S(1)}, u32[]{:S(2)}) copy-start(f32[8,256,256,8]{2,1,3,0:T(8,128)S(1)} %get-tuple-element.894) | copy-start | bytes 50331652 | tf_op jit(solution)/shard_map/cond
  399.3 29.9 %copy-start.26 = (pred[256,256]{0,1:T(8,128)(4,1)S(1)}, pred[256,256]{0,1:T(8,128)(4,1)}, u32[]{:S(2)}) copy-start(pred[256,256]{0,1:T(8,128)(4,1)} %get-tuple-element.994) | copy-start | bytes 196612
  404.1 5.8 %copy-start.8 = (f32[8,256,256,8]{2,1,3,0:T(8,128)}, f32[8,256,256,8]{2,1,3,0:T(8,128)S(1)}, u32[]{:S(2)}) copy-start(f32[8,256,256,8]{2,1,3,0:T(8,128)S(1)} %get-tuple-element.896) | copy-start | bytes 50331652 | tf_op jit(solution)/shard_map/cond
  429.2 30.2 %copy-start.24 = (pred[256,256]{0,1:T(8,128)(4,1)S(1)}, pred[256,256]{0,1:T(8,128)(4,1)}, u32[]{:S(2)}) copy-start(pred[256,256]{0,1:T(8,128)(4,1)} %get-tuple-element.978) | copy-start | bytes 196612
  434.0 5.8 %copy-start.9 = (f32[8,256,256,8]{2,1,3,0:T(8,128)}, f32[8,256,256,8]{2,1,3,0:T(8,128)S(1)}, u32[]{:S(2)}) copy-start(f32[8,256,256,8]{2,1,3,0:T(8,128)S(1)} %get-tuple-element.918) | copy-start | bytes 50331652 | tf_op jit(solution)/shard_map/cond
  459.4 32.8 %copy-start.25 = (pred[256,256]{0,1:T(8,128)(4,1)S(1)}, pred[256,256]{0,1:T(8,128)(4,1)}, u32[]{:S(2)}) copy-start(pred[256,256]{0,1:T(8,128)(4,1)} %get-tuple-element.1010) | copy-start | bytes 196612
  464.2 5.8 %copy-start.10 = (f32[8,256,256,8]{2,1,3,0:T(8,128)}, f32[8,256,256,8]{2,1,3,0:T(8,128)S(1)}, u32[]{:S(2)}) copy-start(f32[8,256,256,8]{2,1,3,0:T(8,128)S(1)} %get-tuple-element.920) | copy-start | bytes 50331652 | tf_op jit(solution)/shard_map/cond
  492.2 0.8 copy-start.23
  493.0 5.3 copy-start.20
  498.3 25.0 %copy-start.22 = (pred[256,256]{0,1:T(8,128)(4,1)S(1)}, pred[256,256]{0,1:T(8,128)(4,1)}, u32[]{:S(2)}) copy-start(pred[256,256]{0,1:T(8,128)(4,1)} %get-tuple-element.1008) | copy-start | bytes 196612
  498.3 25.8 %collective-permute-start.12 = (bf16[8,8,256]{2,1,0:T(8,128)(2,1)S(1)}, bf16[8,8,256]{2,1,0:T(8,128)(2,1)S(1)}, u32[]{:S(2)}, u32[]{:S(2)}) collective-permute-start(bf16[8,8,256]{2,1,0:T(8,128)(2,1)S(1)} %convert_element_type.187), channel_id=1, source_target_pairs={{0,1},{1,0},{2,3},{3,2},{4,5},{5,4},{6,7},{7,6},{8,9},{9,8},{10,11... | collective-permute-start | bytes 98312 | tf_op jit(solution)/shard_map/ppermute | solution.py:19
  523.3 0.8 copy-start.21
where the time goes:
time: 560 us; the launch traced here: 553 us
  matrix products  211 us (38%)
  other arithmetic  119 us (21%)
  local copies, waits for them, and re-layouts  105 us (19%)
  waiting for transfers between devices  66.3 us (12%)
  loops' own time  20.4 us (4%)
  starting transfers between devices  16.9 us (3%)
  between operations  14.8 us (3%)
    dot_general x11, matrix products, update(): jnp.einsum('hgqk,khd->hgqd', weights.astype(jnp.bfloat16), heads_of_value...  145 us
    ppermute x4, waiting for transfers between devices, shifted(): return lax.ppermute(block, axis, route)  66.3 us
    dot_general x11, matrix products, update(): jnp.einsum('qhgd,khd->hgqk', query_tile, heads_of_key, preferred_element_...  65.8 us
    reduce_sum x11, other arithmetic, update(): new_sum = run_sum * factor + jnp.sum(weights, axis=-1)  58.6 us
    cond x28, local copies, waits for them, and re-layouts  44 us
    unnamed x50, local copies, waits for them, and re-layouts  35.7 us
    another operation x18, loops' own time, attend_tile(): return lax.cond(live, update, keep, state)  20.4 us
    convert_element_type x2, other arithmetic, finish(): return jnp.transpose(output, (2, 0, 1, 3)).reshape(block_count, HQ * HEAD...  20 us
  transfers between devices with their start and end apart: 13, of which 3 were waited for; matrix products, arithmetic and copies ran while one was open for 63% of the time, Pallas kernels for 0%

commit v1 on v0

v1 whole, which is shorter than its diff:
```python
import math

import jax
import jax.numpy as jnp
from jax import lax
from jax.experimental import pallas as pl
from jax.experimental.pallas import tpu as pltpu
from jax.sharding import PartitionSpec as P

MESH = pl.DeviceIdType.MESH
HQ = 64
KEY_HEADS = 8
HEAD_SIZE = 128
GROUP = 8
WIDTH = GROUP * HEAD_SIZE
ROWS = 512
TQ = 256
SPAN = 1280
SCALE = math.log2(math.e) / math.sqrt(HEAD_SIZE)
PER_STEP = 4
AHEAD = 3


def tile(t, q_ref, o_ref, kw, vw, bias):
    base = pl.multiple_of(t * TQ, TQ)

    def heads(i, carry):
        for j in range(PER_STEP):
            columns = pl.ds(pl.multiple_of((i * PER_STEP + j) * HEAD_SIZE, HEAD_SIZE), HEAD_SIZE)
            scores = lax.dot_general(
                q_ref[0, :, columns],
                kw[pl.ds(base, SPAN), :],
                (((1,), (1,)), ((), ())),
                preferred_element_type=jnp.float32,
            )
            scores = scores * SCALE + bias[t]
            top = jnp.max(scores, axis=1, keepdims=True)
            weights = jnp.exp2(scores - top).astype(jnp.bfloat16)
            out = jnp.dot(weights, vw[pl.ds(base, SPAN), :], preferred_element_type=jnp.float32)
            o_ref[0, :, columns] = (out[:, :HEAD_SIZE] / out[:, HEAD_SIZE:]).astype(jnp.bfloat16)
        return carry

    lax.fori_loop(0, GROUP // PER_STEP, heads, 0)


def kernel(
    q_ref, own_k, own_v, all_k, all_v, first_ref, o_ref,
    far_k, far_v, near_k, near_v, kw, vw, bias, send, recv,
):
    g = pl.program_id(0)
    t = pl.program_id(1)
    ctx = lax.axis_index("ctx")
    n = lax.axis_size("ctx")
    odd = lax.rem(ctx, 2)
    after = lax.rem(ctx + 2, n)
    before = lax.rem(ctx + n - 2, n)
    beside = ctx + 1 - 2 * odd

    def move(kind, h, source, target, device):
        return pltpu.make_async_remote_copy(
            src_ref=source,
            dst_ref=target.at[h],
            send_sem=send.at[kind, h],
            recv_sem=recv.at[kind, h],
            device_id={"ctx": device},
            device_id_type=MESH,
        )

    def own(ref, h):
        return ref.at[0, :, pl.ds(pl.multiple_of(h * HEAD_SIZE, HEAD_SIZE), HEAD_SIZE)]

    def far(h):
        return (
            move(0, h, own(all_k, h), far_k, after),
            move(1, h, own(all_v, h), far_v, after),
        )

    def near(h):
        return (
            move(2, h, own(all_k, h), near_k, beside),
            move(3, h, own(all_v, h), near_v, beside),
        )

    def relay(h):
        return (
            move(2, h, far_k.at[h], near_k, beside),
            move(3, h, far_v.at[h], near_v, beside),
        )

    def issue(h):
        for copy in far(h):
            copy.start()

        @pl.when(odd == 0)
        def _():
            for copy in near(h):
                copy.start()

    def forward(h):
        for copy in far(h):
            copy.wait_recv()

        @pl.when(odd == 1)
        def _():
            for copy in relay(h):
                copy.start()

    @pl.when((g == 0) & (t == 0))
    def _():
        barrier = pltpu.get_barrier_semaphore()
        for device in (after, before, beside):
            pl.semaphore_signal(barrier, inc=1, device_id={"ctx": device}, device_id_type=MESH)
        pl.semaphore_wait(barrier, 3)
        lax.fori_loop(0, AHEAD, lambda h, c: (issue(h), c)[1], 0)
        vw[:, HEAD_SIZE:] = jnp.ones((3 * ROWS, HEAD_SIZE), jnp.bfloat16)
        for i in range(2):
            column = i * TQ + lax.broadcasted_iota(jnp.int32, (TQ, SPAN), 1)
            row = 2 * ROWS + i * TQ + lax.broadcasted_iota(jnp.int32, (TQ, SPAN), 0)
            first = first_ref[i * TQ : (i + 1) * TQ, :]
            bias[i] = jnp.where((column >= first) & (column <= row), 0.0, -1e30)
        forward(0)

    @pl.when(t == 0)
    def _():
        @pl.when(g + AHEAD < KEY_HEADS)
        def _():
            issue(g + AHEAD)

        for copy in near(g):
            copy.wait_recv()
        kw[:ROWS, :] = far_k[g]
        vw[:ROWS, :HEAD_SIZE] = far_v[g]
        kw[ROWS : 2 * ROWS, :] = near_k[g]
        vw[ROWS : 2 * ROWS, :HEAD_SIZE] = near_v[g]
        kw[2 * ROWS :, :] = own_k[0]
        vw[2 * ROWS :, :HEAD_SIZE] = own_v[0]

    @pl.when((t == 1) & (g + 1 < KEY_HEADS))
    def _():
        forward(g + 1)

    tile(t, q_ref, o_ref, kw, vw, bias)

    @pl.when((g == KEY_HEADS - 1) & (t == 1))
    def _():
        def finish(h, carry):
            for copy in (*far(h), *near(h)):
                copy.wait_send()
            return carry

        lax.fori_loop(0, KEY_HEADS, finish, 0)


def attend(first, queries, keys, values):
    def own(g, t):
        return (0, 0, g)

    return pl.pallas_call(
        kernel,
        grid=(KEY_HEADS, ROWS // TQ),
        in_specs=[
            pl.BlockSpec((1, TQ, WIDTH), lambda g, t: (0, t, g)),
            pl.BlockSpec((1, ROWS, HEAD_SIZE), own),
            pl.BlockSpec((1, ROWS, HEAD_SIZE), own),
            pl.BlockSpec(memory_space=pl.ANY),
            pl.BlockSpec(memory_space=pl.ANY),
            pl.BlockSpec((ROWS, 1), lambda g, t: (0, 0)),
        ],
        out_specs=pl.BlockSpec((1, TQ, WIDTH), lambda g, t: (0, t, g)),
        scratch_shapes=[
            *[pltpu.VMEM((KEY_HEADS, ROWS, HEAD_SIZE), jnp.bfloat16)] * 4,
            pltpu.VMEM((3 * ROWS, HEAD_SIZE), jnp.bfloat16),
            pltpu.VMEM((3 * ROWS, 2 * HEAD_SIZE), jnp.bfloat16),
            pltpu.VMEM((2, TQ, SPAN), jnp.float32),
            pltpu.SemaphoreType.DMA((4, KEY_HEADS)),
            pltpu.SemaphoreType.DMA((4, KEY_HEADS)),
        ],
        out_shape=jax.ShapeDtypeStruct((1, ROWS, HQ * HEAD_SIZE), jnp.bfloat16),
        compiler_params=pltpu.CompilerParams(
            vmem_limit_bytes=50 << 20, collective_id=0, has_side_effects=True
        ),
    )(queries, keys, values, keys, values, first)


def on_device(queries, keys, values, doc_lengths):
    rep = lax.axis_index("rep")
    ctx = lax.axis_index("ctx")
    lengths = lax.dynamic_index_in_dim(doc_lengths, rep, 0, keepdims=False)
    order = jnp.arange(lengths.shape[0])
    starts = jnp.sum(jnp.where(order[None, :] < order[:, None], lengths[None, :], 0), axis=1)
    positions = ctx * ROWS + jnp.arange(ROWS, dtype=jnp.int32)
    first = jnp.max(jnp.where(starts[None, :] <= positions[:, None], starts[None, :], 0), axis=1)
    first = (first - (ctx - 2) * ROWS).astype(jnp.int32)
    return attend(first[:, None], queries, keys, values)


def solution(mesh):
    return jax.shard_map(
        on_device,
        mesh=mesh,
        in_specs=(P("rep", "ctx", None), P("rep", "ctx", None), P("rep", "ctx", None), P()),
        out_specs=P("rep", "ctx", None),
        check_vma=False,
    )
```

time: 560 us -> 122 us (0.22)
  the two profiles are of different devices: /device:TPU:66 before, /device:TPU:0 now
where the time goes in v1:
time: 122 us
  Pallas kernels  111 us (91%)
  local copies, waits for them, and re-layouts  11.1 us (9%)
    pallas_call x1, Pallas kernels, attend(): pl.pallas_call(kernel, grid=(KEY_HEADS, ROWS // TQ), in_specs=[pl.BlockSp...  111 us
    unnamed x7, local copies, waits for them, and re-layouts  10.9 us

profile of v1, /device:TPU:0, one launch (start us, length us, event | category | flops | bytes accessed | tf_op | source)
XLA Modules:
  0.0 122.0 jit_solution(5088591524491365153)
XLA Ops:
  0.0 0.0 copy-start
  0.0 0.7 copy-done
  0.7 0.1 select_reduce_fusion.1
  0.8 0.1 select_reduce_fusion
  0.9 0.1 copy.6.first_ref
  1.1 0.0 copy-start.1
  1.1 1.2 copy-done.1
  2.3 0.0 copy-start.2
  2.3 1.2 %copy-done.2 = bf16[1,512,1024]{2,1,0:T(8,128)(2,1)S(1)} copy-done((bf16[1,512,1024]{2,1,0:T(8,128)(2,1)S(1)}, bf16[1,512,1024]{2,1,0:T(8,128)(2,1)}, u32[]{:S(2)}) %copy-start.2) | copy-done | bytes 1048600
  3.5 110.6 %shard_map.46 = bf16[1,512,8192]{2,1,0:T(8,128)(2,1)} custom-call(bf16[1,512,8192]{2,1,0:T(8,128)(2,1)} %q_ref.1, bf16[1,512,1024]{2,1,0:T(8,128)(2,1)S(1)} %copy-done.1, bf16[1,512,1024]{2,1,0:T(8,128)(2,1)S(1)} %copy-done.2, bf16[1,512,1024]{2,1,0:T(8,128)(2,1)S(1)} %copy-done.1, bf16[1,512,1024]{2,1,0:T(8,128)(2,1)S(1)} %copy-done.2, ...), custom_call_target="tpu_custom_call" | custom-call | tf_op jit(solution)/shard_map/pallas_call | solution.py:158
  114.2 7.8 %copy.8 = bf16[1,512,8192]{2,1,0:T(8,128)(2,1)} copy(bf16[1,512,8192]{2,1,0:T(8,128)(2,1)} %shard_map.46) | data formatting | bytes 16777216
  (3 shorter events, 0.0 us)
Async XLA Ops:
  0.0 0.7 copy-start
  1.1 1.2 %copy-start.1 = (bf16[1,512,1024]{2,1,0:T(8,128)(2,1)S(1)}, bf16[1,512,1024]{2,1,0:T(8,128)(2,1)}, u32[]{:S(2)}) copy-start(bf16[1,512,1024]{2,1,0:T(8,128)(2,1)} %all_k.1) | copy-start | bytes 3145732
  2.3 1.2 %copy-start.2 = (bf16[1,512,1024]{2,1,0:T(8,128)(2,1)S(1)}, bf16[1,512,1024]{2,1,0:T(8,128)(2,1)}, u32[]{:S(2)}) copy-start(bf16[1,512,1024]{2,1,0:T(8,128)(2,1)} %all_v.1) | copy-start | bytes 3145732

commit v2 on v1

v2 whole, which is shorter than its diff:
```python
import math

import jax
import jax.numpy as jnp
from jax import lax
from jax.experimental import pallas as pl
from jax.experimental.pallas import tpu as pltpu
from jax.sharding import PartitionSpec as P

MESH = pl.DeviceIdType.MESH
HQ = 64
KEY_HEADS = 8
HEAD_SIZE = 128
GROUP = 8
WIDTH = GROUP * HEAD_SIZE
ROWS = 512
TQ = 256
SPAN = 1280
SCALE = math.log2(math.e) / math.sqrt(HEAD_SIZE)
AHEAD = 3
PIECE = 128
PIECES = TQ // PIECE
TILES = SPAN // TQ
SLOTS = 4
LAG = 2
STEPS = 2 * KEY_HEADS
FAR_BELOW = -131072.0


def kernel(
    q_ref, q_extra, own_k, own_v, all_k, all_v, k_extra, o_ref,
    far_k, far_v, near_k, near_v, kw, vt, corner, scores, weights, tops, outs, send, recv, sent,
):
    s = pl.program_id(0)
    g = s // 2
    t = lax.rem(s, 2)
    ctx = lax.axis_index("ctx")
    n = lax.axis_size("ctx")
    odd = lax.rem(ctx, 2)
    after = lax.rem(ctx + 2, n)
    before = lax.rem(ctx + n - 2, n)
    beside = ctx + 1 - 2 * odd

    def move(kind, h, source, target, device):
        return pltpu.make_async_remote_copy(
            src_ref=source,
            dst_ref=target.at[h],
            send_sem=send.at[kind, h],
            recv_sem=recv.at[kind, h],
            device_id={"ctx": device},
            device_id_type=MESH,
        )

    def own(ref, h):
        return ref.at[0, :, pl.ds(pl.multiple_of(h * HEAD_SIZE, HEAD_SIZE), HEAD_SIZE)]

    def far(h):
        return (
            move(0, h, own(all_k, h), far_k, after),
            move(1, h, own(all_v, h), far_v, after),
        )

    def near(h):
        return (
            move(2, h, own(all_k, h), near_k, beside),
            move(3, h, own(all_v, h), near_v, beside),
        )

    def relay(h):
        return (
            move(2, h, far_k.at[h], near_k, beside),
            move(3, h, far_v.at[h], near_v, beside),
        )

    def issue(h):
        for copy in far(h):
            copy.start()

        @pl.when(odd == 0)
        def _():
            for copy in near(h):
                copy.start()

    def forward(h):
        for copy in far(h):
            copy.wait_recv()

        @pl.when(odd == 1)
        def _():
            for copy in relay(h):
                copy.start()

    def result(step):
        row = pl.multiple_of(lax.rem(step, 2) * TQ, TQ)
        column = pl.multiple_of(step // 2 * WIDTH, WIDTH)
        slot = lax.rem(step, 3)
        return pltpu.make_async_copy(
            outs.at[slot],
            o_ref.at[0, pl.ds(row, TQ), pl.ds(column, WIDTH)],
            sent.at[slot],
        )

    @pl.when(s == 0)
    def _():
        barrier = pltpu.get_barrier_semaphore()
        for device in (after, before, beside):
            pl.semaphore_signal(barrier, inc=1, device_id={"ctx": device}, device_id_type=MESH)
        pl.semaphore_wait(barrier, 3)
        lax.fori_loop(0, AHEAD, lambda h, c: (issue(h), c)[1], 0)
        kw[:, HEAD_SIZE:] = k_extra[...]
        for i in range(2):
            vt[i, HEAD_SIZE:, :] = jnp.ones((16, 3 * ROWS), jnp.bfloat16)
        below = lax.broadcasted_iota(jnp.int32, (TQ, TQ), 0)
        across = lax.broadcasted_iota(jnp.int32, (TQ, TQ), 1)
        corner[...] = jnp.where(below <= across, 0.0, FAR_BELOW)
        scores[2:] = jnp.zeros((2, SPAN, TQ), jnp.float32)
        tops[...] = jnp.zeros_like(tops)
        forward(0)

    @pl.when((t == 0) & (g < KEY_HEADS))
    def _():
        @pl.when(g + AHEAD < KEY_HEADS)
        def _():
            issue(g + AHEAD)

        for copy in near(g):
            copy.wait_recv()
        slot = lax.rem(g, 2)
        for i, (key, value) in enumerate(
            ((far_k[g], far_v[g]), (near_k[g], near_v[g]), (own_k[0], own_v[0]))
        ):
            kw[i * ROWS : (i + 1) * ROWS, :HEAD_SIZE] = key
            vt[slot, :HEAD_SIZE, i * ROWS : (i + 1) * ROWS] = value.T

    @pl.when((t == 1) & (g + 1 < KEY_HEADS))
    def _():
        forward(g + 1)

    @pl.when(s >= 3)
    def _():
        result(s - 3).wait()

    def work(acc, total):
        def columns(h):
            return slice(h * HEAD_SIZE, (h + 1) * HEAD_SIZE)

        base = pl.multiple_of(t * TQ, TQ)

        def score(h, unit, j, c):
            staged = None
            if j == 0 and c == 0:
                staged = 0
                query = jnp.concatenate([q_ref[0, :, columns(h)], q_extra[...]], axis=1)
                pltpu.matmul_push_rhs(query, 0, unit, transpose=True)
            pltpu.matmul_acc_lhs(
                acc[unit][j % 2][c],
                kw[pl.ds(base + j * TQ + c * PIECE, PIECE), :],
                load_staged_rhs=staged,
            )

        def keep(h, unit, j, c, top):
            part = pltpu.matmul_pop(acc[unit][j % 2][c])
            if j == TILES - 1:
                part = part + corner[c * PIECE : (c + 1) * PIECE, :]
            start = j * TQ + c * PIECE
            scores[h % SLOTS, start : start + PIECE, :] = part
            most = jnp.max(part.reshape(PIECE // 8, 8, TQ), axis=0)
            return most if top is None else jnp.maximum(top, most)

        def weigh(h, unit, j, c, top):
            start = j * TQ + c * PIECE
            part = jnp.exp2((scores[h % SLOTS, start : start + PIECE, :] - top) * SCALE)
            weights[unit, j % 2, c * PIECE : (c + 1) * PIECE, :] = part.astype(jnp.bfloat16)

        def gather(unit, j, at, slot):
            pltpu.matmul_push_rhs(weights[unit, j % 2], 1, unit)
            pltpu.matmul_acc_lhs(
                total[unit],
                vt[slot, :, pl.ds(pl.multiple_of(at + j * TQ, TQ), TQ)],
                load_staged_rhs=1,
            )

        def put(h, unit, out):
            sums = pltpu.matmul_pop(total[unit])
            rows = (sums[:HEAD_SIZE] / sums[HEAD_SIZE : HEAD_SIZE + 1]).T
            outs[out, :, columns(h)] = rows.astype(jnp.bfloat16)

        def step(ahead, behind, unit, top, at, slot, out):
            most = None
            if behind is not None:
                top = jnp.broadcast_to(jnp.max(top, axis=0, keepdims=True), (8, TQ))
                top = jnp.concatenate([top] * (PIECE // 8), axis=0)
            for i in range(TILES * PIECES + PIECES):
                j, c = divmod(i, PIECES)
                if ahead is not None and i < TILES * PIECES:
                    score(ahead, unit, j, c)
                if ahead is not None and 1 <= i <= TILES * PIECES:
                    most = keep(ahead, unit, *divmod(i - 1, PIECES), most)
                if behind is not None and i < TILES * PIECES:
                    weigh(behind, 1 - unit, j, c, top)
                    if c == PIECES - 1:
                        gather(1 - unit, j, at, slot)
            if behind is not None:
                put(behind, 1 - unit, out)
            return most

        last = s - 1 + 3
        old = (
            pl.multiple_of(lax.rem(last + 1, 2) * TQ, TQ),
            lax.rem((last + 1) // 2, 2),
            lax.rem(last, 3),
        )
        new = (base, lax.rem(g, 2), lax.rem(s, 3))

        @pl.when(s < STEPS)
        def _():
            found = {h - GROUP: tops[h - GROUP + LAG] for h in range(GROUP - LAG, GROUP)}
            for h in range(GROUP):
                behind = h - LAG
                where = old if behind < 0 else new
                found[h] = step(h, behind % GROUP, h % 2, found[behind], *where)
            for h in range(GROUP - LAG, GROUP):
                tops[h - GROUP + LAG] = found[h]

        @pl.when(s == STEPS)
        def _():
            for h in range(LAG):
                step(None, GROUP - LAG + h, h % 2, tops[h], *old)

    pl.run_scoped(
        work,
        [
            [[pltpu.ACC(u)((PIECE, TQ), jnp.float32) for _ in range(PIECES)] for _ in range(2)]
            for u in range(2)
        ],
        [pltpu.ACC(u)((HEAD_SIZE + 16, TQ), jnp.float32) for u in range(2)],
    )

    @pl.when(s >= 1)
    def _():
        result(s - 1).start()

    @pl.when(s == STEPS)
    def _():
        def finish(h, carry):
            for copy in (*far(h), *near(h)):
                copy.wait_send()
            return carry

        lax.fori_loop(0, KEY_HEADS, finish, 0)
        result(s - 2).wait()
        result(s - 1).wait()


def attend(q_extra, k_extra, queries, keys, values):
    def head(s):
        return jnp.minimum(s // 2, KEY_HEADS - 1)

    def own(s):
        return (0, 0, head(s))

    return pl.pallas_call(
        kernel,
        grid=(STEPS + 1,),
        in_specs=[
            pl.BlockSpec((1, TQ, WIDTH), lambda s: (0, lax.rem(s, 2), head(s))),
            pl.BlockSpec((TQ, HEAD_SIZE), lambda s: (lax.rem(s, 2), 0)),
            pl.BlockSpec((1, ROWS, HEAD_SIZE), own),
            pl.BlockSpec((1, ROWS, HEAD_SIZE), own),
            pl.BlockSpec(memory_space=pltpu.HBM),
            pl.BlockSpec(memory_space=pltpu.HBM),
            pl.BlockSpec((3 * ROWS, HEAD_SIZE), lambda s: (0, 0)),
        ],
        out_specs=pl.BlockSpec(memory_space=pltpu.HBM),
        scratch_shapes=[
            *[pltpu.VMEM((KEY_HEADS, ROWS, HEAD_SIZE), jnp.bfloat16)] * 4,
            pltpu.VMEM((3 * ROWS, 2 * HEAD_SIZE), jnp.bfloat16),
            pltpu.VMEM((2, HEAD_SIZE + 16, 3 * ROWS), jnp.bfloat16),
            pltpu.VMEM((TQ, TQ), jnp.float32),
            pltpu.VMEM((SLOTS, SPAN, TQ), jnp.float32),
            pltpu.VMEM((2, 2, TQ, TQ), jnp.bfloat16),
            pltpu.VMEM((LAG, 8, TQ), jnp.float32),
            pltpu.VMEM((3, TQ, WIDTH), jnp.bfloat16),
            pltpu.SemaphoreType.DMA((4, KEY_HEADS)),
            pltpu.SemaphoreType.DMA((4, KEY_HEADS)),
            pltpu.SemaphoreType.DMA((3,)),
        ],
        out_shape=jax.ShapeDtypeStruct((1, ROWS, HQ * HEAD_SIZE), jnp.bfloat16),
        compiler_params=pltpu.CompilerParams(
            vmem_limit_bytes=50 << 20, collective_id=0, has_side_effects=True
        ),
    )(queries, q_extra, keys, values, keys, values, k_extra)


def on_device(queries, keys, values, doc_lengths):
    rep = lax.axis_index("rep")
    ctx = lax.axis_index("ctx")
    lengths = lax.dynamic_index_in_dim(doc_lengths, rep, 0, keepdims=False)
    documents = lengths.shape[0]
    order = jnp.arange(documents)
    ends = jnp.sum(jnp.where(order[None, :] <= order[:, None], lengths[None, :], 0), axis=1)
    positions = (ctx - 2) * ROWS + jnp.arange(3 * ROWS, dtype=jnp.int32)
    segment = jnp.sum((positions[:, None] >= ends[None, :]).astype(jnp.int32), axis=1)
    segment = jnp.where(positions < 0, documents, segment)
    same = segment[:, None] == jnp.arange(HEAD_SIZE, dtype=jnp.int32)[None, :]
    k_extra = same.astype(jnp.bfloat16)
    q_extra = jnp.where(same[2 * ROWS :], 0.0, FAR_BELOW).astype(jnp.bfloat16)
    return attend(q_extra, k_extra, queries, keys, values)


def solution(mesh):
    return jax.shard_map(
        on_device,
        mesh=mesh,
        in_specs=(P("rep", "ctx", None), P("rep", "ctx", None), P("rep", "ctx", None), P()),
        out_specs=P("rep", "ctx", None),
        check_vma=False,
    )
```

time: 122 us -> 89.7 us (0.74)
  Pallas kernels: 111 us -> 77.9 us
    pallas_call x1, Pallas kernels: 111 us -> 77.9 us  [attend(): pl.pallas_call(kernel, grid=(STEPS + 1,), in_specs=[pl.BlockSpec((1, TQ,...]
where the time goes in v2:
time: 89.7 us; the launch traced here: 89.4 us
  Pallas kernels  77.9 us (87%)
  local copies, waits for them, and re-layouts  10.9 us (12%)
    pallas_call x1, Pallas kernels, attend(): pl.pallas_call(kernel, grid=(STEPS + 1,), in_specs=[pl.BlockSpec((1, TQ,...  77.9 us
    unnamed x7, local copies, waits for them, and re-layouts  10.9 us

profile of v2, /device:TPU:0, one launch (start us, length us, event | category | flops | bytes accessed | tf_op | source)
XLA Modules:
  0.0 89.4 jit_solution(17769202086747769575)
XLA Ops:
  0.0 0.0 copy-start
  0.0 0.7 copy-done
  0.7 0.1 select_reduce_fusion
  0.8 0.1 convert_reduce_fusion
  0.9 0.3 fusion
  1.3 0.0 copy-start.1
  1.3 1.2 %copy-done.1 = bf16[1,512,1024]{2,1,0:T(8,128)(2,1)S(1)} copy-done((bf16[1,512,1024]{2,1,0:T(8,128)(2,1)S(1)}, bf16[1,512,1024]{2,1,0:T(8,128)(2,1)}, u32[]{:S(2)}) %copy-start.1) | copy-done | bytes 1048600
  2.5 0.0 copy-start.2
  2.5 1.2 %copy-done.2 = bf16[1,512,1024]{2,1,0:T(8,128)(2,1)S(1)} copy-done((bf16[1,512,1024]{2,1,0:T(8,128)(2,1)S(1)}, bf16[1,512,1024]{2,1,0:T(8,128)(2,1)}, u32[]{:S(2)}) %copy-start.2) | copy-done | bytes 1048600
  3.7 77.9 %shard_map.46 = bf16[1,512,8192]{2,1,0:T(8,128)(2,1)} custom-call(bf16[1,512,8192]{2,1,0:T(8,128)(2,1)} %q_ref.1, bf16[512,128]{1,0:T(8,128)(2,1)S(1)} %select_convert_fusion.q_extra, bf16[1,512,1024]{2,1,0:T(8,128)(2,1)S(1)} %copy-done.1, bf16[1,512,1024]{2,1,0:T(8,128)(2,1)S(1)} %copy-done.2, bf16[1,512,1024]{2,1,0:T(8,128)(2,1)S(1)} %copy-done.1, ...), custom_call_target="tpu_custom_call" | custom-call | tf_op jit(solution)/shard_map/pallas_call | solution.py:262
  81.6 7.8 %copy.6 = bf16[1,512,8192]{2,1,0:T(8,128)(2,1)} copy(bf16[1,512,8192]{2,1,0:T(8,128)(2,1)} %shard_map.46) | data formatting | bytes 16777216
  (4 shorter events, 0.1 us)
Async XLA Ops:
  0.0 0.7 copy-start
  1.3 1.2 %copy-start.1 = (bf16[1,512,1024]{2,1,0:T(8,128)(2,1)S(1)}, bf16[1,512,1024]{2,1,0:T(8,128)(2,1)}, u32[]{:S(2)}) copy-start(bf16[1,512,1024]{2,1,0:T(8,128)(2,1)} %all_k.1) | copy-start | bytes 3145732
  2.5 1.2 %copy-start.2 = (bf16[1,512,1024]{2,1,0:T(8,128)(2,1)S(1)}, bf16[1,512,1024]{2,1,0:T(8,128)(2,1)}, u32[]{:S(2)}) copy-start(bf16[1,512,1024]{2,1,0:T(8,128)(2,1)} %all_v.1) | copy-start | bytes 3145732

commit v3 on v2

--- a/solution.py
+++ b/solution.py
@@ -22,14 +22,14 @@
 PIECES = TQ // PIECE
 TILES = SPAN // TQ
 SLOTS = 4
-LAG = 2
+LAG = 3
 STEPS = 2 * KEY_HEADS
 FAR_BELOW = -131072.0
 
 
 def kernel(
     q_ref, q_extra, own_k, own_v, all_k, all_v, k_extra, o_ref,
-    far_k, far_v, near_k, near_v, kw, vt, corner, scores, weights, tops, outs, send, recv, sent,
+    far_k, far_v, near_k, near_v, kw, vt, corner, scores, tops, outs, send, recv, sent,
 ):
     s = pl.program_id(0)
     g = s // 2
@@ -113,7 +113,7 @@
         below = lax.broadcasted_iota(jnp.int32, (TQ, TQ), 0)
         across = lax.broadcasted_iota(jnp.int32, (TQ, TQ), 1)
         corner[...] = jnp.where(below <= across, 0.0, FAR_BELOW)
-        scores[2:] = jnp.zeros((2, SPAN, TQ), jnp.float32)
+        scores[SLOTS - LAG :] = jnp.zeros((LAG, SPAN, TQ), jnp.float32)
         tops[...] = jnp.zeros_like(tops)
         forward(0)
 
@@ -170,10 +170,10 @@
         def weigh(h, unit, j, c, top):
             start = j * TQ + c * PIECE
             part = jnp.exp2((scores[h % SLOTS, start : start + PIECE, :] - top) * SCALE)
-            weights[unit, j % 2, c * PIECE : (c + 1) * PIECE, :] = part.astype(jnp.bfloat16)
-
-        def gather(unit, j, at, slot):
-            pltpu.matmul_push_rhs(weights[unit, j % 2], 1, unit)
+            return part.astype(jnp.bfloat16)
+
+        def gather(unit, j, at, slot, parts):
+            pltpu.matmul_push_rhs(jnp.concatenate(parts, axis=0), 1, unit)
             pltpu.matmul_acc_lhs(
                 total[unit],
                 vt[slot, :, pl.ds(pl.multiple_of(at + j * TQ, TQ), TQ)],
@@ -197,9 +197,10 @@
                 if ahead is not None and 1 <= i <= TILES * PIECES:
                     most = keep(ahead, unit, *divmod(i - 1, PIECES), most)
                 if behind is not None and i < TILES * PIECES:
-                    weigh(behind, 1 - unit, j, c, top)
+                    parts = [] if c == 0 else parts
+                    parts.append(weigh(behind, 1 - unit, j, c, top))
                     if c == PIECES - 1:
-                        gather(1 - unit, j, at, slot)
+                        gather(1 - unit, j, at, slot, parts)
             if behind is not None:
                 put(behind, 1 - unit, out)
             return most
@@ -278,7 +279,6 @@
             pltpu.VMEM((2, HEAD_SIZE + 16, 3 * ROWS), jnp.bfloat16),
             pltpu.VMEM((TQ, TQ), jnp.float32),
             pltpu.VMEM((SLOTS, SPAN, TQ), jnp.float32),
-            pltpu.VMEM((2, 2, TQ, TQ), jnp.bfloat16),
             pltpu.VMEM((LAG, 8, TQ), jnp.float32),
             pltpu.VMEM((3, TQ, WIDTH), jnp.bfloat16),
             pltpu.SemaphoreType.DMA((4, KEY_HEADS)),
@@ -287,7 +287,7 @@
         ],
         out_shape=jax.ShapeDtypeStruct((1, ROWS, HQ * HEAD_SIZE), jnp.bfloat16),
         compiler_params=pltpu.CompilerParams(
-            vmem_limit_bytes=50 << 20, collective_id=0, has_side_effects=True
+            vmem_limit_bytes=63 << 20, collective_id=0, has_side_effects=True
         ),
     )(queries, q_extra, keys, values, keys, values, k_extra)
 

time: 89.7 us -> 82.5 us (0.920)
  Pallas kernels: 77.9 us -> 71.9 us
  local copies, waits for them, and re-layouts: 10.9 us -> 8.48 us
  other arithmetic: 0.53 us -> 1.93 us
    pallas_call x1, Pallas kernels: 77.9 us -> 71.9 us  [attend(): pl.pallas_call(kernel, grid=(STEPS + 1,), in_specs=[pl.BlockSpec((1, TQ,...]
    unnamed x7 -> x3, local copies, waits for them, and re-layouts: 10.9 us -> 8.47 us
where the time goes in v3:
time: 82.5 us; the launch traced here: 82.3 us
  Pallas kernels  71.9 us (87%)
  local copies, waits for them, and re-layouts  8.48 us (10%)
  other arithmetic  1.93 us (2%)
    pallas_call x1, Pallas kernels, attend(): pl.pallas_call(kernel, grid=(STEPS + 1,), in_specs=[pl.BlockSpec((1, TQ,...  71.9 us
    unnamed x3, local copies, waits for them, and re-layouts  8.47 us

profile of v3, /device:TPU:0, one launch (start us, length us, event | category | flops | bytes accessed | tf_op | source)
XLA Modules:
  0.0 82.3 jit_solution(4923914609309157551)
XLA Ops:
  0.0 0.0 copy-start
  0.0 0.7 copy-done
  0.7 0.1 select_reduce_fusion
  0.8 0.1 convert_reduce_fusion
  0.9 1.0 %fusion = (bf16[1536,128]{1,0:T(8,128)(2,1)}, pred[1536,128]{1,0:T(8,128)(4,1)S(1)}) fusion(s32[1536]{0:T(1024)S(1)} %compare_select_fusion), kind=kLoop, calls=%fused_computation.7 | loop fusion | flops 393216 | bytes 595968 | tf_op jit(solution)/shard_map/convert_element_type | solution.py:306
  2.0 0.7 select_convert_fusion.q_extra
  2.7 71.9 %shard_map.46 = bf16[1,512,8192]{2,1,0:T(8,128)(2,1)} custom-call(bf16[1,512,8192]{2,1,0:T(8,128)(2,1)} %q_ref.1, bf16[512,128]{1,0:T(8,128)(2,1)} %select_convert_fusion.q_extra, bf16[1,512,1024]{2,1,0:T(8,128)(2,1)} %all_k.1, bf16[1,512,1024]{2,1,0:T(8,128)(2,1)} %all_v.1, bf16[1,512,1024]{2,1,0:T(8,128)(2,1)} %all_k.1, bf16[1,512,1024]{2,1,0:T(8,128)(2,1)} %all_v.1, ...), custom_call_target="tpu_custom_call" | custom-call | tf_op jit(solution)/shard_map/pallas_call | solution.py:263
  74.5 7.8 %copy.6 = bf16[1,512,8192]{2,1,0:T(8,128)(2,1)} copy(bf16[1,512,8192]{2,1,0:T(8,128)(2,1)} %shard_map.46) | data formatting | bytes 16777216
  (3 shorter events, 0.0 us)
Async XLA Ops:
  0.0 0.7 copy-start

commit v4 on v3

--- a/solution.py
+++ b/solution.py
@@ -28,8 +28,8 @@
 
 
 def kernel(
-    q_ref, q_extra, own_k, own_v, all_k, all_v, k_extra, o_ref,
-    far_k, far_v, near_k, near_v, kw, vt, corner, scores, tops, outs, send, recv, sent,
+    q_ref, bounds, own_k, own_v, all_k, all_v, o_ref,
+    far_k, far_v, near_k, near_v, kw, vt, q_extra, corner, scores, tops, outs, send, recv, sent,
 ):
     s = pl.program_id(0)
     g = s // 2
@@ -107,7 +107,12 @@
             pl.semaphore_signal(barrier, inc=1, device_id={"ctx": device}, device_id_type=MESH)
         pl.semaphore_wait(barrier, 3)
         lax.fori_loop(0, AHEAD, lambda h, c: (issue(h), c)[1], 0)
-        kw[:, HEAD_SIZE:] = k_extra[...]
+        place = lax.broadcasted_iota(jnp.int32, (3 * ROWS, HEAD_SIZE), 0) + (ctx - 2) * ROWS
+        same = (place >= bounds[0:1, :]) & (place < bounds[1:2, :])
+        kw[:, HEAD_SIZE:] = jnp.where(same, 1.0, 0.0).astype(jnp.bfloat16)
+        place = lax.broadcasted_iota(jnp.int32, (ROWS, HEAD_SIZE), 0) + ctx * ROWS
+        same = (place >= bounds[0:1, :]) & (place < bounds[1:2, :])
+        q_extra[...] = jnp.where(same, 0.0, FAR_BELOW).astype(jnp.bfloat16)
         for i in range(2):
             vt[i, HEAD_SIZE:, :] = jnp.ones((16, 3 * ROWS), jnp.bfloat16)
         below = lax.broadcasted_iota(jnp.int32, (TQ, TQ), 0)
@@ -145,12 +150,13 @@
             return slice(h * HEAD_SIZE, (h + 1) * HEAD_SIZE)
 
         base = pl.multiple_of(t * TQ, TQ)
+        extra = q_extra[pl.ds(base, TQ), :]
 
         def score(h, unit, j, c):
             staged = None
             if j == 0 and c == 0:
                 staged = 0
-                query = jnp.concatenate([q_ref[0, :, columns(h)], q_extra[...]], axis=1)
+                query = jnp.concatenate([q_ref[0, :, columns(h)], extra], axis=1)
                 pltpu.matmul_push_rhs(query, 0, unit, transpose=True)
             pltpu.matmul_acc_lhs(
                 acc[unit][j % 2][c],
@@ -253,7 +259,7 @@
         result(s - 1).wait()
 
 
-def attend(q_extra, k_extra, queries, keys, values):
+def attend(bounds, queries, keys, values):
     def head(s):
         return jnp.minimum(s // 2, KEY_HEADS - 1)
 
@@ -265,18 +271,18 @@
         grid=(STEPS + 1,),
         in_specs=[
             pl.BlockSpec((1, TQ, WIDTH), lambda s: (0, lax.rem(s, 2), head(s))),
-            pl.BlockSpec((TQ, HEAD_SIZE), lambda s: (lax.rem(s, 2), 0)),
+            pl.BlockSpec((8, HEAD_SIZE), lambda s: (0, 0)),
             pl.BlockSpec((1, ROWS, HEAD_SIZE), own),
             pl.BlockSpec((1, ROWS, HEAD_SIZE), own),
             pl.BlockSpec(memory_space=pltpu.HBM),
             pl.BlockSpec(memory_space=pltpu.HBM),
-            pl.BlockSpec((3 * ROWS, HEAD_SIZE), lambda s: (0, 0)),
         ],
         out_specs=pl.BlockSpec(memory_space=pltpu.HBM),
         scratch_shapes=[
             *[pltpu.VMEM((KEY_HEADS, ROWS, HEAD_SIZE), jnp.bfloat16)] * 4,
             pltpu.VMEM((3 * ROWS, 2 * HEAD_SIZE), jnp.bfloat16),
             pltpu.VMEM((2, HEAD_SIZE + 16, 3 * ROWS), jnp.bfloat16),
+            pltpu.VMEM((ROWS, HEAD_SIZE), jnp.bfloat16),
             pltpu.VMEM((TQ, TQ), jnp.float32),
             pltpu.VMEM((SLOTS, SPAN, TQ), jnp.float32),
             pltpu.VMEM((LAG, 8, TQ), jnp.float32),
@@ -289,23 +295,23 @@
         compiler_params=pltpu.CompilerParams(
             vmem_limit_bytes=63 << 20, collective_id=0, has_side_effects=True
         ),
-    )(queries, q_extra, keys, values, keys, values, k_extra)
+    )(queries, bounds, keys, values, keys, values)
 
 
 def on_device(queries, keys, values, doc_lengths):
     rep = lax.axis_index("rep")
-    ctx = lax.axis_index("ctx")
     lengths = lax.dynamic_index_in_dim(doc_lengths, rep, 0, keepdims=False)
     documents = lengths.shape[0]
-    order = jnp.arange(documents)
-    ends = jnp.sum(jnp.where(order[None, :] <= order[:, None], lengths[None, :], 0), axis=1)
-    positions = (ctx - 2) * ROWS + jnp.arange(3 * ROWS, dtype=jnp.int32)
-    segment = jnp.sum((positions[:, None] >= ends[None, :]).astype(jnp.int32), axis=1)
-    segment = jnp.where(positions < 0, documents, segment)
-    same = segment[:, None] == jnp.arange(HEAD_SIZE, dtype=jnp.int32)[None, :]
-    k_extra = same.astype(jnp.bfloat16)
-    q_extra = jnp.where(same[2 * ROWS :], 0.0, FAR_BELOW).astype(jnp.bfloat16)
-    return attend(q_extra, k_extra, queries, keys, values)
+    order = jnp.arange(documents)[None, :]
+    lane = jnp.arange(HEAD_SIZE)[:, None]
+    starts = jnp.sum(jnp.where(order < lane, lengths[None, :], 0), axis=1)
+    ends = jnp.sum(jnp.where(order <= lane, lengths[None, :], 0), axis=1)
+    outside = lane[:, 0] == documents
+    starts = jnp.where(outside, -(1 << 20), starts)
+    ends = jnp.where(outside, 0, ends)
+    bounds = jnp.broadcast_to(jnp.stack([starts, ends])[None], (4, 2, HEAD_SIZE))
+    bounds = bounds.reshape(8, HEAD_SIZE).astype(jnp.int32)
+    return attend(bounds, queries, keys, values)
 
 
 def solution(mesh):

time: 82.5 us -> 81.2 us (0.984)
  other arithmetic: 1.93 us -> 0.11 us
    convert_element_type x2 -> x0, other arithmetic: 1.71 us -> none  [the longest x1 1.02 us: on_device(): k_extra = same.astype(jnp.bfloat16)]
where the time goes in v4:
time: 81.2 us; the launch traced here: 81 us
  Pallas kernels  71.8 us (88%)
  local copies, waits for them, and re-layouts  9.07 us (11%)
    pallas_call x1, Pallas kernels, attend(): pl.pallas_call(kernel, grid=(STEPS + 1,), in_specs=[pl.BlockSpec((1, TQ,...  71.8 us
    unnamed x3, local copies, waits for them, and re-layouts  8.47 us

profile of v4, /device:TPU:0, one launch (start us, length us, event | category | flops | bytes accessed | tf_op | source)
XLA Modules:
  0.0 81.0 jit_solution(13905161561315628391)
XLA Ops:
  0.0 0.0 copy-start
  0.0 0.7 copy-done
  0.7 0.1 select_reduce_fusion.1
  0.8 0.6 broadcast_in_dim.40
  1.4 71.8 %shard_map.46 = bf16[1,512,8192]{2,1,0:T(8,128)(2,1)} custom-call(bf16[1,512,8192]{2,1,0:T(8,128)(2,1)} %q_ref.1, s32[8,128]{1,0:T(8,128)} %bitcast.7, bf16[1,512,1024]{2,1,0:T(8,128)(2,1)} %all_k.1, bf16[1,512,1024]{2,1,0:T(8,128)(2,1)} %all_v.1, bf16[1,512,1024]{2,1,0:T(8,128)(2,1)} %all_k.1, bf16[1,512,1024]{2,1,0:T(8,128)(2,1)} %all_v.1), custom_call_target="tpu_custom_call" | custom-call | tf_op jit(solution)/shard_map/pallas_call | solution.py:269
  73.2 7.8 %copy.6 = bf16[1,512,8192]{2,1,0:T(8,128)(2,1)} copy(bf16[1,512,8192]{2,1,0:T(8,128)(2,1)} %shard_map.46) | data formatting | bytes 16777216
  (3 shorter events, 0.0 us)
Async XLA Ops:
  0.0 0.7 copy-start
